TPU v7x, 32 devices: a whole 2x2x4 slice. The times are simulated.
32 devices in a mesh: dp: 8 (over z, y), section: 4 (over x, core).
Axes of the slice: x: 2, y: 2, z: 4, core: 2. Of those that a mesh axis runs over, the one named last changes fastest.
Arguments:
- hidden_in: bfloat16 [4096, 768], P('dp'), may hold values from -6 to 6
- out_grad: float32 [4096, 768], P('dp'), may hold values from -6 to 6
- seq_counts: int32 [8, 2], P('dp'), may hold values from 1 to 2, as said below
- segment_ids: int32 [32, 128], P('dp'), may hold values from 0 to 3, never falling along the last dimension, each value on 1 to 64 neighbouring positions
- proj: bfloat16 [4, 768, 3072], P('section'), may hold values from -8 to 8
- proj_master: float32 [4, 768, 3072], P('section', 'dp'), may hold values from -8 to 8
- proj_m: float32 [4, 768, 3072], P('section', 'dp'), may hold values from -5 to 5
- proj_v: float32 [4, 768, 3072], P('section', 'dp'), may hold values from 0.01 to 10
- down: bfloat16 [2, 3072, 768], P(None, 'section'), may hold values from -0.109375 to 0.109375
- down_master: float32 [2, 3072, 768], P(None, 'section', 'dp'), may hold values from -0.109375 to 0.109375
- down_m: float32 [2, 3072, 768], P(None, 'section', 'dp'), may hold values from -5 to 5
- down_v: float32 [2, 3072, 768], P(None, 'section', 'dp'), may hold values from 0.01 to 10
- vectors: float32 [2, 12, 768], replicated, may hold values from -1 to 1.5
- vec_m: float32 [2, 12, 768], replicated, may hold values from -5 to 5
- vec_v: float32 [2, 12, 768], replicated, may hold values from 0.01 to 10
Outputs:
- section_out: bfloat16 [4, 4096, 768], P('section', 'dp')
- section_in_grad: float32 [4, 4096, 768], P('section', 'dp')
- proj_grad: float32 [4, 768, 3072], P('section', 'dp')
- proj_master_new: float32 [4, 768, 3072], P('section', 'dp')
- proj_m_new: float32 [4, 768, 3072], P('section', 'dp')
- proj_v_new: float32 [4, 768, 3072], P('section', 'dp')
- proj_copy: bfloat16 [4, 768, 3072], P('section')
- down_grad: float32 [2, 3072, 768], P(None, 'section', 'dp')
- down_master_new: float32 [2, 3072, 768], P(None, 'section', 'dp')
- down_m_new: float32 [2, 3072, 768], P(None, 'section', 'dp')
- down_v_new: float32 [2, 3072, 768], P(None, 'section', 'dp')
- down_copy: bfloat16 [2, 3072, 768], P(None, 'section')
- vec_grad: float32 [2, 12, 768], replicated
- vec_m_new: float32 [2, 12, 768], replicated
- vec_v_new: float32 [2, 12, 768], replicated
Inputs may be any that keep to these rules, and one draw needn't show every extreme that they name: The first seq_counts[g, b] slots of micro-batch b of group g are live; some micro-batch of some group is full. `segment_ids`: document numbers never fall along a sequence; each document has 1 to 64 tokens.
All inputs are finite; a program needn't handle non-finite values.
Results may differ from a plain program's by a relative error of at most 0.02.
Values may be sent and summed in bfloat16 or wider, within the bound.
No kernel may reach another device: no remote copies, remote signals or barrier semaphores. Data moves between devices by JAX's collectives and lax.ppermute only.
A program may use at most 1.875 GiB of HBM per device.

v0:
```python
import math

import jax
import jax.numpy as jnp
from jax import lax
from jax.sharding import PartitionSpec as P

HEADS = 12


norm_eps = 1e-05
beta_one = 0.9
beta_two = 0.98
adam_eps = 1e-06
learn_rate = 0.001
weight_decay = 0.01
adam_step = 100.0


def from_behind(block, axis, distance):
    devices = range(lax.axis_size(axis))
    route = [(i - distance, i) for i in devices if i - distance in devices]
    return lax.ppermute(block, axis, route)


def norm_forward(residual_sum, gain, shift):
    centered = residual_sum - jnp.mean(residual_sum, -1, keepdims=True)
    scale_inv = lax.rsqrt(jnp.mean(centered * centered, -1, keepdims=True) + norm_eps)
    normed = centered * scale_inv
    return (normed * gain + shift, normed, scale_inv)


def norm_backward(upstream, normed, scale_inv, gain):
    scaled = upstream * gain
    inner = scale_inv * (
        scaled
        - jnp.mean(scaled, -1, keepdims=True)
        - normed * jnp.mean(scaled * normed, -1, keepdims=True)
    )
    return (inner, jnp.sum(upstream * normed, 0), jnp.sum(upstream, 0))


def right_dot(left_side, weight_now):
    return lax.dot_general(
        left_side, weight_now, (((1,), (1,)), ((), ())), preferred_element_type=jnp.float32
    )


def left_dot(left_side, other_side):
    return lax.dot_general(
        left_side, other_side, (((0,), (0,)), ((), ())), preferred_element_type=jnp.float32
    )


def gelu_slope(pre_act):
    return 0.5 * (1.0 + jax.scipy.special.erf(pre_act / math.sqrt(2.0))) + pre_act * jnp.exp(
        -0.5 * pre_act * pre_act
    ) / math.sqrt(2.0 * math.pi)


def attend_forward(hidden, documents, matrices, vector_rows):
    seq_count, seq_len, model_width = hidden.shape
    head_size = model_width // HEADS
    score_scale = head_size ** (-0.5)
    flat_rows = hidden.reshape(-1, model_width)
    joined_bias = jnp.concatenate([vector_rows[0], jnp.zeros_like(vector_rows[0]), vector_rows[1]])
    joined_proj = (
        jnp.dot(flat_rows, matrices[:, : 3 * model_width], preferred_element_type=jnp.float32)
        + joined_bias
    )
    packed = joined_proj.astype(jnp.bfloat16).reshape(seq_count, seq_len, 3, HEADS, head_size)
    queries = packed[:, :, 0]
    keys_part = packed[:, :, 1]
    values = packed[:, :, 2]
    scores = (
        jnp.einsum("sqhd,skhd->shqk", queries, keys_part, preferred_element_type=jnp.float32)
        * score_scale
    )
    same_doc = (documents[:, :, None] == documents[:, None, :])[:, None]
    scores = jnp.where(same_doc, scores, -1e30)
    exponent = jnp.exp(scores - jnp.max(scores, -1, keepdims=True))
    attn_probs = exponent / jnp.sum(exponent, -1, keepdims=True)
    probs_low = attn_probs.astype(jnp.bfloat16)
    context = jnp.einsum("shqk,skhd->sqhd", probs_low, values, preferred_element_type=jnp.float32)
    context = context.astype(jnp.bfloat16).reshape(-1, model_width)
    branch_out = (
        jnp.dot(context, matrices[:, 3 * model_width :], preferred_element_type=jnp.float32)
        + vector_rows[2]
    )
    residual_sum = flat_rows.astype(jnp.float32) + branch_out
    output, normed, scale_inv = norm_forward(residual_sum, vector_rows[3], vector_rows[4])
    saved_parts = (
        flat_rows,
        queries,
        keys_part,
        values,
        attn_probs,
        probs_low,
        context,
        normed,
        scale_inv,
    )
    return (output.reshape(hidden.shape), saved_parts)


def attend_backward(hidden, documents, matrices, vector_rows, upstream):
    model_width = hidden.shape[-1]
    score_scale = (model_width // HEADS) ** (-0.5)
    flat_rows, queries, keys_part, values, attn_probs, probs_low, context, normed, scale_inv = (
        attend_forward(hidden, documents, matrices, vector_rows)[1]
    )
    grad_sum, grad_gain, grad_shift = norm_backward(
        upstream.reshape(-1, model_width), normed, scale_inv, vector_rows[3]
    )
    grad_branch = grad_sum.astype(jnp.bfloat16)
    grad_out_weight = left_dot(context, grad_branch)
    grad_context = (
        right_dot(grad_branch, matrices[:, 3 * model_width :])
        .astype(jnp.bfloat16)
        .reshape(queries.shape)
    )
    grad_values = jnp.einsum(
        "shqk,sqhd->skhd", probs_low, grad_context, preferred_element_type=jnp.float32
    ).astype(jnp.bfloat16)
    grad_probs = jnp.einsum(
        "sqhd,skhd->shqk", grad_context, values, preferred_element_type=jnp.float32
    )
    grad_scores = (
        attn_probs * (grad_probs - jnp.sum(attn_probs * grad_probs, -1, keepdims=True))
    ).astype(jnp.bfloat16)
    grad_queries = (
        jnp.einsum("shqk,skhd->sqhd", grad_scores, keys_part, preferred_element_type=jnp.float32)
        * score_scale
    ).astype(jnp.bfloat16)
    grad_keys = (
        jnp.einsum("shqk,sqhd->skhd", grad_scores, queries, preferred_element_type=jnp.float32)
        * score_scale
    ).astype(jnp.bfloat16)
    grad_joined = jnp.stack([grad_queries, grad_keys, grad_values], 2).reshape(-1, 3 * model_width)
    grad_input = right_dot(grad_joined, matrices[:, : 3 * model_width]) + grad_sum
    grad_matrices = jnp.concatenate([left_dot(flat_rows, grad_joined), grad_out_weight], 1)
    bias_sums = jnp.sum(grad_joined.astype(jnp.float32), 0)
    grad_vectors = jnp.concatenate(
        [
            jnp.stack(
                [
                    bias_sums[:model_width],
                    bias_sums[2 * model_width :],
                    jnp.sum(grad_branch.astype(jnp.float32), 0),
                    grad_gain,
                    grad_shift,
                ]
            ),
            jnp.zeros((7, model_width), jnp.float32),
        ]
    )
    return (grad_input.reshape(hidden.shape), grad_matrices, grad_vectors)


def feed_forward(hidden, matrices, down_layer, vector_rows):
    model_width = hidden.shape[-1]
    flat_rows = hidden.reshape(-1, model_width)
    pre_act = jnp.dot(flat_rows, matrices, preferred_element_type=jnp.float32) + vector_rows[
        5:9
    ].reshape(-1)
    gelu_low = jax.nn.gelu(pre_act, approximate=False).astype(jnp.bfloat16)
    branch_out = jnp.dot(gelu_low, down_layer, preferred_element_type=jnp.float32) + vector_rows[9]
    residual_sum = flat_rows.astype(jnp.float32) + branch_out
    output, normed, scale_inv = norm_forward(residual_sum, vector_rows[10], vector_rows[11])
    return (output.reshape(hidden.shape), (flat_rows, pre_act, gelu_low, normed, scale_inv))


def feed_backward(hidden, matrices, down_layer, vector_rows, upstream):
    model_width = hidden.shape[-1]
    flat_rows, pre_act, gelu_low, normed, scale_inv = feed_forward(
        hidden, matrices, down_layer, vector_rows
    )[1]
    grad_sum, grad_gain, grad_shift = norm_backward(
        upstream.reshape(-1, model_width), normed, scale_inv, vector_rows[10]
    )
    grad_branch = grad_sum.astype(jnp.bfloat16)
    grad_down = left_dot(gelu_low, grad_branch)
    grad_gelu = right_dot(grad_branch, down_layer)
    grad_pre = (grad_gelu * gelu_slope(pre_act)).astype(jnp.bfloat16)
    grad_input = right_dot(grad_pre, matrices) + grad_sum
    grad_matrices = left_dot(flat_rows, grad_pre)
    grad_vectors = jnp.concatenate(
        [
            jnp.zeros((5, model_width), jnp.float32),
            jnp.sum(grad_pre.astype(jnp.float32), 0).reshape(-1, model_width),
            jnp.stack([jnp.sum(grad_branch.astype(jnp.float32), 0), grad_gain, grad_shift]),
        ]
    )
    return (grad_input.reshape(hidden.shape), grad_matrices, grad_down, grad_vectors)


def adam_apply(weight_now, first_moment, second_moment, gradient, decay_rate):
    first_new = beta_one * first_moment + (1.0 - beta_one) * gradient
    second_new = beta_two * second_moment + (1.0 - beta_two) * gradient * gradient
    update = (
        first_new
        / (1.0 - beta_one**adam_step)
        / (jnp.sqrt(second_new / (1.0 - beta_two**adam_step)) + adam_eps)
    )
    return (weight_now - learn_rate * (update + decay_rate * weight_now), first_new, second_new)


def shards(
    hidden_in,
    out_grad,
    seq_counts,
    segment_ids,
    proj,
    proj_master,
    proj_m,
    proj_v,
    down,
    down_master,
    down_m,
    down_v,
    vectors,
    vec_m,
    vec_v,
):
    section_count = lax.axis_size("section")
    group_count = lax.axis_size("dp")
    section_index = lax.axis_index("section")
    model_width = hidden_in.shape[1]
    micro_count = seq_counts.shape[1]
    seq_len = segment_ids.shape[1]
    slot_count = segment_ids.shape[0] // micro_count
    inputs = hidden_in.reshape(micro_count, slot_count, seq_len, model_width)
    cotangent = out_grad.reshape(micro_count, slot_count, seq_len, model_width)
    documents = segment_ids.reshape(micro_count, slot_count, seq_len)
    live_counts = seq_counts[0]
    layer_index = section_index // 2
    is_attention = section_index % 2 == 0
    matrices = proj[0]
    down_whole = lax.all_gather(down, "section", axis=1, tiled=True)
    down_layer = lax.dynamic_index_in_dim(down_whole, layer_index, 0, keepdims=False)
    vector_rows = lax.dynamic_index_in_dim(vectors, layer_index, 0, keepdims=False)

    def sub_forward(hidden, docs_block):
        return lax.cond(
            is_attention,
            lambda: attend_forward(hidden, docs_block, matrices, vector_rows)[0],
            lambda: feed_forward(hidden, matrices, down_layer, vector_rows)[0],
        )

    def attend_branch(hidden, docs_block, upstream):
        grad_input, grad_matrices, grad_vectors = attend_backward(
            hidden, docs_block, matrices, vector_rows, upstream
        )
        return (grad_input, grad_matrices, jnp.zeros(down_layer.shape, jnp.float32), grad_vectors)

    def sub_backward(hidden, docs_block, upstream):
        return lax.cond(
            is_attention,
            lambda: attend_branch(hidden, docs_block, upstream),
            lambda: feed_backward(hidden, matrices, down_layer, vector_rows, upstream),
        )

    def zero_grads():
        return (
            jnp.zeros(matrices.shape, jnp.float32),
            jnp.zeros(down_layer.shape, jnp.float32),
            jnp.zeros(vector_rows.shape, jnp.float32),
        )

    def micro_forward(hidden, docs_block, live_count):
        live_mask = lax.broadcasted_iota(jnp.int32, (hidden.shape[0], 1, 1), 0) < live_count
        return jnp.where(live_mask, sub_forward(hidden, docs_block), 0.0).astype(jnp.bfloat16)

    def micro_backward(hidden, docs_block, live_count, upstream):
        live_mask = lax.broadcasted_iota(jnp.int32, (hidden.shape[0], 1, 1), 0) < live_count
        return sub_backward(hidden, docs_block, jnp.where(live_mask, upstream, 0.0))

    kept_inputs = jnp.zeros(inputs.shape, jnp.bfloat16)
    produced = jnp.zeros(inputs.shape, jnp.bfloat16)
    incoming = jnp.zeros(inputs.shape[1:], jnp.bfloat16)
    for step_number in range(micro_count + section_count - 1):
        micro_index = step_number - section_index
        active = (micro_index >= 0) & (micro_index < micro_count)
        micro_slot = jnp.clip(micro_index, 0, micro_count - 1)
        own_input = lax.dynamic_index_in_dim(inputs, micro_slot, 0, keepdims=False)
        hidden = jnp.where(section_index == 0, own_input, incoming)
        docs_block = lax.dynamic_index_in_dim(documents, micro_slot, 0, keepdims=False)
        live_count = lax.dynamic_index_in_dim(live_counts, micro_slot, 0, keepdims=False)
        result = lax.cond(
            active,
            lambda: micro_forward(hidden, docs_block, live_count),
            lambda: jnp.zeros(hidden.shape, jnp.bfloat16),
        )
        kept_inputs = jnp.where(
            active, lax.dynamic_update_index_in_dim(kept_inputs, hidden, micro_slot, 0), kept_inputs
        )
        produced = jnp.where(
            active, lax.dynamic_update_index_in_dim(produced, result, micro_slot, 0), produced
        )
        incoming = from_behind(result, "section", 1)
    acc_matrices, acc_down, acc_vectors = zero_grads()
    in_grads = jnp.zeros(inputs.shape, jnp.float32)
    returning = jnp.zeros(inputs.shape[1:], jnp.bfloat16)
    for step_number in range(micro_count + section_count - 1):
        micro_index = step_number - (section_count - 1 - section_index)
        active = (micro_index >= 0) & (micro_index < micro_count)
        micro_slot = jnp.clip(micro_index, 0, micro_count - 1)
        own_cotangent = lax.dynamic_index_in_dim(cotangent, micro_slot, 0, keepdims=False)
        upstream = jnp.where(
            section_index == section_count - 1, own_cotangent, returning.astype(jnp.float32)
        )
        hidden = lax.dynamic_index_in_dim(kept_inputs, micro_slot, 0, keepdims=False)
        docs_block = lax.dynamic_index_in_dim(documents, micro_slot, 0, keepdims=False)
        live_count = lax.dynamic_index_in_dim(live_counts, micro_slot, 0, keepdims=False)
        grad_input, grad_matrices, grad_down, grad_vectors = lax.cond(
            active,
            lambda: micro_backward(hidden, docs_block, live_count, upstream),
            lambda: (jnp.zeros(hidden.shape, jnp.float32),) + zero_grads(),
        )
        acc_matrices = acc_matrices + grad_matrices
        acc_down = acc_down + grad_down
        acc_vectors = acc_vectors + grad_vectors
        in_grads = jnp.where(
            active, lax.dynamic_update_index_in_dim(in_grads, grad_input, micro_slot, 0), in_grads
        )
        returning = from_behind(grad_input.astype(jnp.bfloat16), "section", -1)
    down_local = lax.dynamic_update_index_in_dim(
        jnp.zeros(down_whole.shape, jnp.float32), acc_down, layer_index, 0
    )
    down_part = lax.psum_scatter(
        down_local.astype(jnp.bfloat16), "section", scatter_dimension=1, tiled=True
    )
    down_grad = (
        lax.psum_scatter(down_part, "dp", scatter_dimension=2, tiled=True).astype(jnp.float32)
        / group_count
    )
    vector_local = lax.dynamic_update_index_in_dim(
        jnp.zeros(vectors.shape, jnp.float32), acc_vectors, layer_index, 0
    )
    vec_grad = lax.psum(vector_local, ("dp", "section")) / group_count
    matrix_local = acc_matrices[None]
    matrix_sum = lax.psum(matrix_local.astype(jnp.bfloat16), "dp").astype(jnp.float32)
    share_rows = model_width // group_count
    share_start = lax.axis_index("dp") * share_rows
    proj_grad = lax.dynamic_slice_in_dim(matrix_sum, share_start, share_rows, 1) / group_count
    proj_new, proj_m_new, proj_v_new = adam_apply(
        proj_master, proj_m, proj_v, proj_grad, weight_decay
    )
    down_new, down_m_new, down_v_new = adam_apply(
        down_master, down_m, down_v, down_grad, weight_decay
    )
    vec_moments = adam_apply(vectors, vec_m, vec_v, vec_grad, 0.0)
    proj_copy, down_copy = (
        lax.all_gather(proj_new.astype(jnp.bfloat16), "dp", axis=1, tiled=True),
        lax.all_gather(down_new.astype(jnp.bfloat16), "dp", axis=2, tiled=True),
    )
    section_out = produced.reshape(1, -1, model_width)
    section_in_grad = in_grads.reshape(1, -1, model_width)
    return (
        section_out,
        section_in_grad,
        proj_grad,
        proj_new,
        proj_m_new,
        proj_v_new,
        proj_copy,
        down_grad,
        down_new,
        down_m_new,
        down_v_new,
        down_copy,
        vec_grad,
        vec_moments[1],
        vec_moments[2],
    )


def solution(mesh):
    placed = (
        P("dp", None),
        P("dp", None),
        P("dp", None),
        P("dp", None),
        P("section", None, None),
        P("section", "dp", None),
        P("section", "dp", None),
        P("section", "dp", None),
        P(None, "section", None),
        P(None, "section", "dp"),
        P(None, "section", "dp"),
        P(None, "section", "dp"),
        P(),
        P(),
        P(),
    )
    return jax.shard_map(
        shards,
        mesh=mesh,
        in_specs=placed,
        out_specs=(
            P("section", "dp", None),
            P("section", "dp", None),
            P("section", "dp", None),
            P("section", "dp", None),
            P("section", "dp", None),
            P("section", "dp", None),
            P("section", None, None),
            P(None, "section", "dp"),
            P(None, "section", "dp"),
            P(None, "section", "dp"),
            P(None, "section", "dp"),
            P(None, "section", None),
            P(),
            P(),
            P(),
        ),
        check_vma=False,
    )
```

profile of v0, /device:TPU:0, one launch (start us, length us, event | category | flops | bytes accessed | tf_op | source)
XLA Modules:
  0.0 3181.0 jit_solution(13852356133159821372)
XLA Ops:
  8.5 68.1 %all-gather.4.cloned.1.call-done = bf16[2,3072,768]{2,1,0:T(8,128)(2,1)} async-done(((bf16[2,768,768]{2,1,0:T(8,128)(2,1)}), bf16[2,3072,768]{2,1,0:T(8,128)(2,1)}) %all-gather.4.cloned.1.call-update) | async-done | bytes 9437200 | tf_op jit(solution)/shard_map/all_gather | solution.py:239
  81.5 21.4 conditional.20
  82.8 18.1 conditional
  105.9 21.5 conditional.21
  107.2 18.3 conditional.1
  140.7 18.9 collective-permute-start.2
  162.1 10.0 conditional.23
  181.7 19.7 conditional.25
  203.9 26.2 collective-permute-done.4
  231.0 19.4 conditional.26
  262.5 19.6 conditional.27
  284.6 139.7 %collective-permute-done.6 = bf16[2,128,768]{2,1,0:T(8,128)(2,1)S(1)} collective-permute-done((bf16[2,128,768]{2,1,0:T(8,128)(2,1)S(1)}, bf16[2,128,768]{2,1,0:T(8,128)(2,1)S(1)}, u32[]{:S(2)}, u32[]{:S(2)}) %collective-permute-start.6) | collective-permute-done | bytes 393248 | tf_op jit(solution)/shard_map/ppermute | solution.py:23
  425.2 81.5 %conditional.28 = (f32[2,128,768]{2,1,0:T(8,128)}, f32[12,768]{1,0:T(8,128)}, f32[768,3072]{1,0:T(8,128)}, f32[3072,768]{0,1:T(8,128)}) conditional(s32[]{:T(128)} %convert_element_type.684, () %tuple.233, (pred[]{:T(512)}, bf16[2,2,128,768]{3,2,1,0:T(8,128)(2,1)S(1)}, s32[]{:T(128)}, s32[1,2]{1,0:T(1,128)S(1)}, ...), branch_computations={%region_119.120_spmd, %region_120.142_spmd} | conditional | flops 7315385344 | bytes 161420768 | solution.py:315
  428.6 58.6 %conditional.8 = (f32[2,128,768]{2,1,0:T(8,128)}, f32[768,3072]{0,1:T(8,128)}, f32[3072,768]{1,0:T(8,128)}, f32[12,768]{1,0:T(8,128)}) conditional(s32[]{:T(128)} %convert_element_type.623, (bf16[2,128,768]{2,1,0:T(8,128)(2,1)}, bf16[768,3072]{1,0:T(8,128)(2,1)}, f32[12,768]{1,0:T(8,128)S(1)}, bf16[3072,768]{1,0:T(8,128)(2,1)}, ...), branch_computations={%region_121.129_spmd, %region_130.141_spmd} | conditional | flops 7314992128 | bytes 120329552 | solution.py:257
  487.3 9.6 copy.596
  496.9 9.7 copy.598
  516.2 68.2 %conditional.29 = (f32[12,768]{1,0:T(8,128)}, f32[1,2,128,768]{3,2,1,0:T(8,128)}, f32[768,3072]{1,0:T(8,128)}, f32[3072,768]{0,1:T(8,128)}) conditional(s32[]{:T(128)} %convert_element_type.687, () %tuple.235, (pred[]{:T(512)}, bf16[2,2,128,768]{3,2,1,0:T(8,128)(2,1)S(1)}, s32[]{:T(128)}, s32[1,2]{1,0:T(1,128)S(1)}, ...), branch_computations={%region_142.143_spmd, %region_143.165_spmd} | conditional | flops 7315385344 | bytes 147264832 | solution.py:315
  519.7 45.4 %conditional.9 = (f32[768,3072]{0,1:T(8,128)}, f32[3072,768]{1,0:T(8,128)}, f32[12,768]{1,0:T(8,128)}, f32[1,2,128,768]{3,2,1,0:T(8,128)}) conditional(s32[]{:T(128)} %convert_element_type.646, (bf16[2,128,768]{2,1,0:T(8,128)(2,1)}, bf16[768,3072]{1,0:T(8,128)(2,1)}, f32[12,768]{1,0:T(8,128)S(1)}, bf16[3072,768]{1,0:T(8,128)(2,1)}, ...), branch_computations={%region_144.152_spmd, %region_153.164_spmd} | conditional | flops 7314992128 | bytes 106173600 | solution.py:257
  565.1 9.6 copy.600
  574.6 9.7 copy.602
  584.4 16.1 add_add_fusion
  612.9 134.9 %dynamic_update_slice.25 = bf16[2,3072,768]{1,0,2:T(2,128)(2,1)} dynamic-update-slice(bf16[2,3072,768]{1,0,2:T(2,128)(2,1)} %broadcast_in_dim.473, bf16[1,3072,768]{1,0,2:T(2,128)(2,1)} %broadcast_in_dim.474, s32[]{:T(128)S(6)} %select_n.391, s32[]{:T(128)} %constant.1387.clone.1, s32[]{:T(128)} %constant.1387.clone.1) | dynamic-update-slice | bytes 9437188 | tf_op jit(solution)/shard_map/jit(dynamic_update_index_in_dim)/dynamic_update_slice | solution.py:327
  747.8 419.0 %copy.581 = bf16[2,3072,768]{0,2,1:T(8,128)(2,1)} copy(bf16[2,3072,768]{1,0,2:T(2,128)(2,1)} %dynamic_update_slice.25) | data formatting | bytes 18874368
  1166.9 966.8 %reshape.975 = bf16[3072,1536]{1,0:T(8,128)(2,1)} reshape(bf16[3072,768,2]{2,1,0:T(8,128)(2,1)} %bitcast.199) | data formatting | bytes 18874368
  2133.7 22.6 fusion.606
  2156.3 55.9 %reduce-scatter.4.cloned.1.call-done = bf16[768,1536]{1,0:T(8,128)(2,1)} async-done(((bf16[3072,1536]{1,0:T(8,128)(2,1)}), bf16[768,1536]{1,0:T(8,128)(2,1)}) %reduce-scatter.4.cloned.1.call-update) | async-done | bytes 2359312
  2212.3 326.0 %reshape.976 = bf16[768,768,2]{2,1,0:T(8,128)(2,1)} reshape(bf16[768,1536]{1,0:T(8,128)(2,1)} %reduce-scatter.4.cloned.1.call-done) | data formatting | bytes 4718592
  2538.2 133.9 %copy.582 = bf16[2,768,768]{1,0,2:T(2,128)(2,1)} copy(bf16[2,768,768]{0,2,1:T(8,128)(2,1)} %bitcast.200) | data formatting | bytes 4718592
  2676.5 230.4 %all-reduce.7.cloned.1.call-done = (bf16[1,768,3072]{2,1,0:T(8,128)(2,1)}, bf16[2,768,768]{1,0,2:T(2,128)(2,1)}) async-done(((bf16[1,768,3072]{2,1,0:T(8,128)(2,1)}, bf16[2,768,768]{1,0,2:T(2,128)(2,1)}), (bf16[1,768,3072]{2,1,0:T(8,128)(2,1)}, bf16[2,768,768]{1,0,2:T(2,128)(2,1)})) %all-reduce.7.cloned.1.call-update) | async-done | bytes 7077904 | tf_op jit(solution)/shard_map/psum | solution.py:342
  2925.6 105.7 %all-reduce.5.cloned.1.call-done = f32[2,12,768]{2,0,1:T(2,128)} async-done(((f32[2,12,768]{2,0,1:T(2,128)}), f32[2,12,768]{2,0,1:T(2,128)}) %all-reduce.5.cloned.1.call-update) | async-done | bytes 73744 | tf_op jit(solution)/shard_map/psum | solution.py:340
  3033.0 55.1 %all-gather.8.cloned.1.call-done = bf16[2,768,768]{1,0,2:T(2,128)(2,1)} async-done(((bf16[2,768,96]{1,0,2:T(2,128)(2,1)}), bf16[2,768,768]{1,0,2:T(2,128)(2,1)}) %all-gather.8.cloned.1.call-update) | async-done | bytes 2359312 | tf_op jit(solution)/shard_map/all_gather | solution.py:355
  3094.9 74.0 %all-gather.6.cloned.1.call-done = bf16[1,768,3072]{2,1,0:T(8,128)(2,1)} async-done(((bf16[1,96,3072]{2,1,0:T(8,128)(2,1)}), bf16[1,768,3072]{2,1,0:T(8,128)(2,1)}) %all-gather.6.cloned.1.call-update) | async-done | bytes 4718608 | tf_op jit(solution)/shard_map/all_gather | solution.py:354
  (304 shorter events, 298.3 us)
Async XLA Ops:
  7.2 69.4 %all-gather.4.cloned.1.call-start = ((), (), s32[]{:S(2)}) async-start(), calls=%async_computation.1 | async-start | bytes 11796480 | tf_op jit(solution)/shard_map/all_gather | solution.py:239
  7.9 2204.3 %reduce-scatter.4.cloned.1.call-start = ((), (), s32[]{:S(2)}) async-start(), calls=%async_computation.5 | async-start | bytes 11796480
  8.1 508.1 %copy-start.31 = (f32[1,12,768]{2,1,0:T(8,128)}, f32[1,12,768]{2,1,0:T(8,128)S(1)}, u32[]{:S(2)}) copy-start(f32[1,12,768]{2,1,0:T(8,128)S(1)} %copy.1011) | copy-start | bytes 110596
  8.5 73.0 %copy-start.94 = (s32[4,128]{1,0:T(4,128)S(1)}, s32[4,128]{1,0:T(4,128)}, u32[]{:S(2)}) copy-start(s32[4,128]{1,0:T(4,128)} %param.58) | copy-start | bytes 6148
  8.5 73.0 %copy-start.96 = (s32[1,2]{1,0:T(1,128)S(1)}, s32[1,2]{1,0:T(1,128)}, u32[]{:S(2)}) copy-start(s32[1,2]{1,0:T(1,128)} %param.57) | copy-start | bytes 28
  102.9 2.8 collective-permute-start
  127.4 4.4 collective-permute-start.1
  140.7 20.5 collective-permute-start.2
  162.1 19.6 copy-start.3
  172.2 8.5 collective-permute-start.3
  202.5 27.5 collective-permute-start.4
  251.5 10.1 collective-permute-start.5
  283.3 141.0 %collective-permute-start.6 = (bf16[2,128,768]{2,1,0:T(8,128)(2,1)S(1)}, bf16[2,128,768]{2,1,0:T(8,128)(2,1)S(1)}, u32[]{:S(2)}, u32[]{:S(2)}) collective-permute-start(bf16[2,128,768]{2,1,0:T(8,128)(2,1)S(1)} %convert_element_type.685), channel_id=1, source_target_pairs={{1,0},{2,1},{3,2},{5,4},{6,5},{7,6},{9,8},{10,9},{11,10},{13,12},{... | collective-permute-start | bytes 1179656 | tf_op jit(solution)/shard_map/ppermute | solution.py:23
  447.9 2.7 copy-start.52
  453.8 3.2 copy-start.73
  459.1 6.6 copy-start.14
  465.7 4.2 copy-start.15
  465.7 4.2 copy-start.53
  507.9 7.4 collective-permute-start.7
  534.9 3.2 copy-start.75
  2133.7 773.2 %all-reduce.7.cloned.1.call-start = ((), (), s32[]{:S(2)}) async-start(), calls=%async_computation.6 | async-start | bytes 14155776 | tf_op jit(solution)/shard_map/psum | solution.py:342
  2672.1 236.0 %copy-start.69 = (f32[2,768,96]{1,2,0:T(8,128)S(1)}, f32[2,768,96]{1,2,0:T(8,128)}, u32[]{:S(2)}) copy-start(f32[2,768,96]{1,2,0:T(8,128)} %param.64) | copy-start | bytes 1769476
  2672.1 359.2 %all-reduce.5.cloned.1.call-start = ((), (), s32[]{:S(2)}) async-start(), calls=%async_computation.4 | async-start | bytes 147456 | tf_op jit(solution)/shard_map/psum | solution.py:340
  2675.8 236.6 %copy-start.67 = (f32[1,96,3072]{2,1,0:T(8,128)S(1)}, f32[1,96,3072]{2,1,0:T(8,128)}, u32[]{:S(2)}) copy-start(f32[1,96,3072]{2,1,0:T(8,128)} %param.60) | copy-start | bytes 3538948
  2675.8 236.6 %copy-start.68 = (f32[1,96,3072]{2,1,0:T(8,128)S(1)}, f32[1,96,3072]{2,1,0:T(8,128)}, u32[]{:S(2)}) copy-start(f32[1,96,3072]{2,1,0:T(8,128)} %param.61) | copy-start | bytes 3538948
  2676.4 411.7 %all-gather.8.cloned.1.call-start = ((), (), s32[]{:S(2)}) async-start(), calls=%async_computation.3 | async-start | bytes 2654208 | tf_op jit(solution)/shard_map/all_gather | solution.py:355
  2912.1 256.8 %all-gather.6.cloned.1.call-start = ((), (), s32[]{:S(2)}) async-start(), calls=%async_computation.2 | async-start | bytes 5308416 | tf_op jit(solution)/shard_map/all_gather | solution.py:354
  2920.0 3.0 copy-start.16
  2921.6 109.8 %copy-start.92 = (f32[2,12,768]{2,0,1:T(2,128)S(1)}, f32[2,12,768]{2,0,1:T(2,128)}, u32[]{:S(2)}) copy-start(f32[2,12,768]{2,0,1:T(2,128)} %param.69) | copy-start | bytes 221188
  2921.6 109.8 %copy-start.93 = (f32[2,12,768]{2,0,1:T(2,128)S(1)}, f32[2,12,768]{2,0,1:T(2,128)}, u32[]{:S(2)}) copy-start(f32[2,12,768]{2,0,1:T(2,128)} %param.68) | copy-start | bytes 221188
  2925.6 248.1 %copy-start.2 = (f32[2,2,128,768]{3,2,1,0:T(8,128)}, f32[2,2,128,768]{3,2,1,0:T(8,128)S(1)}, u32[]{:S(2)}) copy-start(f32[2,2,128,768]{3,2,1,0:T(8,128)S(1)} %select_dynamic-update-slice_fusion) | copy-start | bytes 4718596
  3168.9 4.9 copy-start.1
  (20 other events, 34.9 us)
Sparse Core Ops, SparseCore 0:
  9.6 66.9 all-gather.3
  2133.8 78.4 reduce-scatter.3
  2672.3 234.5 all-reduce.6
  2913.8 117.4 all-reduce.4
  3034.2 53.9 all-gather.7
  3090.4 78.4 all-gather.5
where the time goes:
time: 3220 us; the launch traced here: 3180 us
  local copies, waits for them, and re-layouts  2140 us (66%)
  waiting for transfers between devices  776 us (24%)
  other arithmetic  97.3 us (3%)
  matrix products  69.9 us (2%)
  loops' own time  43.9 us (1%)
  starting transfers between devices  36.3 us (1%)
    unnamed x49, local copies, waits for them, and re-layouts  1860 us
    psum x1, waiting for transfers between devices, shards(): lax.psum(matrix_local.astype(jnp.bfloat16), 'dp').astype(jnp.float32)  230 us
    ppermute x8, waiting for transfers between devices, from_behind(): return lax.ppermute(block, axis, route)  186 us
    dynamic_update_slice x1, local copies, waits for them, and re-layouts, shards(): lax.dynamic_update_index_in_dim(jnp.zeros(down_whole.shape, jnp.float32),...  135 us
    psum x1, waiting for transfers between devices, shards(): vec_grad = lax.psum(vector_local, ('dp', 'section')) / group_count  106 us
    all_gather x1, waiting for transfers between devices, shards(): lax.all_gather(proj_new.astype(jnp.bfloat16), 'dp', axis=1, tiled=True)  74 us
    all_gather x1, waiting for transfers between devices, shards(): down_whole = lax.all_gather(down, 'section', axis=1, tiled=True)  68.1 us
  transfers between devices with their start and end apart: 14, of which 14 were waited for; matrix products, arithmetic and copies ran while one was open for 2% of the time, Pallas kernels for 0%

commit v1 on v0

v1 whole, which is shorter than its diff:
```python
import functools
import math

import jax
import jax.numpy as jnp
from jax import lax
from jax.experimental import pallas as pl
from jax.experimental.pallas import tpu as pltpu
from jax.sharding import PartitionSpec as P

HEADS = 12
HEAD_PAIRS = HEADS // 2

norm_eps = 1e-05
beta_one = 0.9
beta_two = 0.98
adam_eps = 1e-06
learn_rate = 0.001
weight_decay = 0.01
adam_step = 100.0

VMEM_LIMIT = 56 * 1024 * 1024
low = jnp.bfloat16
full = jnp.float32

vmem = pl.BlockSpec(memory_space=pltpu.VMEM)
smem = pl.BlockSpec(memory_space=pltpu.SMEM)
anywhere = pl.BlockSpec(memory_space=pl.ANY)


def dot(a, b):
    return lax.dot_general(a, b, (((1,), (0,)), ((), ())), preferred_element_type=full)


def dot_right(a, b):
    return lax.dot_general(a, b, (((1,), (1,)), ((), ())), preferred_element_type=full)


def dot_left(a, b):
    return lax.dot_general(a, b, (((0,), (0,)), ((), ())), preferred_element_type=full)


def row_mean(z):
    return jnp.mean(z, -1, keepdims=True)


def norm_rows(z):
    centered = z - row_mean(z)
    inv = lax.rsqrt(row_mean(centered * centered) + norm_eps)
    return centered * inv, inv


def norm_rows_back(upstream, normed, inv, gain):
    scaled = upstream * gain
    return inv * (scaled - row_mean(scaled) - normed * row_mean(scaled * normed))


def live_rows(rows, live_count, seq_len):
    return lax.broadcasted_iota(jnp.int32, (rows, 1), 0) < live_count * seq_len


def column_sum(block):
    return jnp.sum(block, 0, keepdims=True)


def call(kernel, outs, ins, specs, scratch=(), flops=0, moved=0):
    return pl.pallas_call(
        kernel,
        out_shape=outs,
        in_specs=specs,
        out_specs=jax.tree.map(lambda _: vmem, outs),
        scratch_shapes=list(scratch),
        compiler_params=pltpu.CompilerParams(vmem_limit_bytes=VMEM_LIMIT),
        cost_estimate=pl.CostEstimate(flops=flops, bytes_accessed=moved, transcendentals=0),
    )(*ins)


def pair_masks(seq_len):
    first = lax.broadcasted_iota(jnp.int32, (seq_len, 128), 1) < 64
    return first


def spread_pair(block, first):
    zero = jnp.zeros_like(block)
    return jnp.concatenate([jnp.where(first, block, zero), jnp.where(first, zero, block)], 0)


def pair_probs(q, keys_two, same_doc, scale, seq_len):
    scores = dot_right(q, keys_two) * scale
    parts = []
    for half in range(2):
        part = jnp.where(same_doc, scores[:, half * seq_len : (half + 1) * seq_len], -1e30)
        exponent = jnp.exp(part - jnp.max(part, -1, keepdims=True))
        parts.append(exponent / jnp.sum(exponent, -1, keepdims=True))
    return parts


def pick_weights(core, own_hbm, other_hbm, attn_buf, feed_buf, sems):
    if attn_buf is not None:
        @pl.when(core == 0)
        def _():
            pltpu.make_async_copy(own_hbm, attn_buf, sems.at[0]).start()

        @pl.when(core != 0)
        def _():
            pltpu.make_async_copy(other_hbm, attn_buf, sems.at[0]).start()

    if feed_buf is not None:
        @pl.when(core == 0)
        def _():
            pltpu.make_async_copy(other_hbm, feed_buf, sems.at[1]).start()

        @pl.when(core != 0)
        def _():
            pltpu.make_async_copy(own_hbm, feed_buf, sems.at[1]).start()


def forward_first(
    scal, h_ref, doc_row, doc_col, vec, own_hbm, other_hbm,
    qkv_ref, ctx_ref, n_ref, r_ref, h_next, act_ref, slope_ref,
    attn_buf, feed_buf, sems,
):
    rows, width = h_ref.shape
    seq_len = doc_row.shape[1]
    seqs = rows // seq_len
    scale = (width // HEADS) ** (-0.5)
    pick_weights(scal[0], own_hbm, other_hbm, attn_buf, feed_buf, sems)
    hidden = h_ref[...]
    pltpu.make_async_copy(own_hbm, attn_buf, sems.at[0]).wait()
    for part in range(3):
        cols = slice(part * width, (part + 1) * width)
        block = dot(hidden, attn_buf[:, cols])
        if part == 0:
            block = block + vec[0:1, :]
        if part == 2:
            block = block + vec[1:2, :]
        qkv_ref[:, cols] = block.astype(low)
    first = pair_masks(seq_len)
    for s in range(seqs):
        at = slice(s * seq_len, (s + 1) * seq_len)
        same_doc = doc_col[at, :] == doc_row[s : s + 1, :]
        for p in range(HEAD_PAIRS):
            q = qkv_ref[at, p * 128 : (p + 1) * 128]
            keys_two = spread_pair(qkv_ref[at, width + p * 128 : width + (p + 1) * 128], first)
            values_two = spread_pair(
                qkv_ref[at, 2 * width + p * 128 : 2 * width + (p + 1) * 128], first
            )
            probs = pair_probs(q, keys_two, same_doc, scale, seq_len)
            probs_low = jnp.concatenate([x.astype(low) for x in probs], 1)
            ctx_ref[at, p * 128 : (p + 1) * 128] = dot(probs_low, values_two).astype(low)
    z = hidden.astype(full) + (dot(ctx_ref[...], attn_buf[:, 3 * width :]) + vec[2:3, :])
    normed, inv = norm_rows(z)
    n_ref[...] = normed
    r_ref[...] = inv
    live = live_rows(rows, scal[2], seq_len)
    nxt = jnp.where(live, normed * vec[3:4, :] + vec[4:5, :], 0.0).astype(low)
    h_next[...] = nxt
    pltpu.make_async_copy(own_hbm, feed_buf, sems.at[1]).wait()
    for k in range(4):
        pre = dot(nxt, feed_buf[:, k * width : (k + 1) * width]) + vec[5 + k : 6 + k, :]
        half_cdf = 0.5 * (1.0 + lax.erf(pre * (1.0 / math.sqrt(2.0))))
        act_ref[k] = (pre * half_cdf).astype(low)
        slope_ref[k] = (
            half_cdf + pre * jnp.exp(-0.5 * pre * pre) * (1.0 / math.sqrt(2.0 * math.pi))
        ).astype(slope_ref.dtype)


def forward_second(scal, h_ref, act_ref, vec, d0, d1, d2, d3, h_next, n_ref, r_ref, *, seq_len):
    rows, width = h_ref.shape
    section = scal[1]
    total = h_ref[...].astype(full) + vec[9:10, :]
    for m, block in enumerate((d0, d1, d2, d3)):
        total = total + dot(act_ref[section ^ m], block[...])
    normed, inv = norm_rows(total)
    n_ref[...] = normed
    r_ref[...] = inv
    live = live_rows(rows, scal[2], seq_len)
    h_next[...] = jnp.where(live, normed * vec[10:11, :] + vec[11:12, :], 0.0).astype(low)


def backward_second(
    scal, e_ref, n_ref, r_ref, slope_ref, vec, d0, d1, d2, d3, own_hbm, other_hbm,
    db_ref, dpre_ref, dh_ref, sums, feed_buf, sems, *, seq_len,
):
    rows, width = n_ref.shape
    section = scal[1]
    pick_weights(scal[0], own_hbm, other_hbm, None, feed_buf, sems)
    upstream = jnp.where(live_rows(rows, scal[2], seq_len), e_ref[...], 0.0)
    normed = n_ref[...]
    dz = norm_rows_back(upstream, normed, r_ref[...], vec[10:11, :])
    db = dz.astype(low)
    db_ref[...] = db
    sums[4:5, :] = column_sum(db.astype(full))
    sums[5:6, :] = column_sum(upstream * normed)
    sums[6:7, :] = column_sum(upstream)
    sums[7:8, :] = jnp.zeros((1, width), full)
    for m, block in enumerate((d0, d1, d2, d3)):
        at = section ^ m
        dact = dot_right(db, block[...])
        dpre = (dact * slope_ref[at].astype(full)).astype(low)
        dpre_ref[at] = dpre
    total = dz
    pltpu.make_async_copy(own_hbm, feed_buf, sems.at[1]).wait()
    for k in range(4):
        dpre = dpre_ref[k]
        sums[k : k + 1, :] = column_sum(dpre.astype(full))
        total = total + dot_right(dpre, feed_buf[:, k * width : (k + 1) * width])
    dh_ref[...] = total


def backward_first(
    scal, e_ref, n_ref, r_ref, qkv_ref, doc_row, doc_col, vec, own_hbm, other_hbm,
    dqkvd_ref, dh_ref, sums, attn_buf, dctx_buf, sems,
):
    rows, width = n_ref.shape
    seq_len = doc_row.shape[1]
    seqs = rows // seq_len
    scale = (width // HEADS) ** (-0.5)
    pick_weights(scal[0], own_hbm, other_hbm, attn_buf, None, sems)
    upstream = e_ref[...].astype(low).astype(full)
    upstream = jnp.where(live_rows(rows, scal[2], seq_len), upstream, 0.0)
    normed = n_ref[...]
    dz = norm_rows_back(upstream, normed, r_ref[...], vec[3:4, :])
    da = dz.astype(low)
    dqkvd_ref[3] = da
    sums[2:3, :] = column_sum(da.astype(full))
    sums[3:4, :] = column_sum(upstream * normed)
    sums[4:5, :] = column_sum(upstream)
    sums[5:8, :] = jnp.zeros((3, width), full)
    pltpu.make_async_copy(own_hbm, attn_buf, sems.at[0]).wait()
    dctx_buf[...] = dot_right(da, attn_buf[:, 3 * width :]).astype(low)
    first = pair_masks(seq_len)
    for s in range(seqs):
        at = slice(s * seq_len, (s + 1) * seq_len)
        same_doc = doc_col[at, :] == doc_row[s : s + 1, :]
        for p in range(HEAD_PAIRS):
            here = slice(p * 128, (p + 1) * 128)
            q = qkv_ref[at, here]
            keys_two = spread_pair(qkv_ref[at, width + p * 128 : width + (p + 1) * 128], first)
            values_two = spread_pair(
                qkv_ref[at, 2 * width + p * 128 : 2 * width + (p + 1) * 128], first
            )
            dctx = dctx_buf[at, here]
            probs = pair_probs(q, keys_two, same_doc, scale, seq_len)
            probs_low = jnp.concatenate([x.astype(low) for x in probs], 1)
            dv_two = dot_left(probs_low, dctx)
            dqkvd_ref[2, at, here] = jnp.where(
                first, dv_two[:seq_len, :], dv_two[seq_len:, :]
            ).astype(low)
            dprobs = dot_right(dctx, values_two)
            dscores = []
            for half in range(2):
                part = dprobs[:, half * seq_len : (half + 1) * seq_len]
                inner = jnp.sum(probs[half] * part, -1, keepdims=True)
                dscores.append((probs[half] * (part - inner)).astype(low))
            dscores = jnp.concatenate(dscores, 1)
            dqkvd_ref[0, at, here] = (dot(dscores, keys_two) * scale).astype(low)
            dk_two = dot_left(dscores, q)
            dqkvd_ref[1, at, here] = (
                jnp.where(first, dk_two[:seq_len, :], dk_two[seq_len:, :]) * scale
            ).astype(low)
    total = dz
    for k in range(3):
        block = dqkvd_ref[k]
        if k != 1:
            sums[k // 2 : k // 2 + 1, :] = column_sum(block.astype(full))
        total = total + dot_right(block, attn_buf[:, k * width : (k + 1) * width])
    dh_ref[...] = total


def down_gradient(act_own, act_other, db_own, db_other, out):
    for t in range(2):
        out[t] = (
            dot_left(db_own[...], act_own[t]) + dot_left(db_other[...], act_other[t])
        ).astype(low)


def weight_gradient(left_own, left_other, right_own, right_other, out):
    out[...] = (
        dot_left(left_own[...], right_own[...]) + dot_left(left_other[...], right_other[...])
    ).astype(low)


def swap(block, axis, mask):
    return lax.ppermute(block, axis, [(i, i ^ mask) for i in range(lax.axis_size(axis))])


def adam_apply(weight_now, first_moment, second_moment, gradient, decay_rate):
    first_new = beta_one * first_moment + (1.0 - beta_one) * gradient
    second_new = beta_two * second_moment + (1.0 - beta_two) * gradient * gradient
    update = (
        first_new
        / (1.0 - beta_one**adam_step)
        / (jnp.sqrt(second_new / (1.0 - beta_two**adam_step)) + adam_eps)
    )
    return (weight_now - learn_rate * (update + decay_rate * weight_now), first_new, second_new)


def masks_of(count):
    return [1 << b for b in range(count.bit_length() - 1)]


def pick(block, at):
    return lax.dynamic_index_in_dim(block, at, 1, keepdims=False)


class Exchange:
    def __init__(self):
        self.count = lax.axis_size("dp")
        self.index = lax.axis_index("dp")
        self.masks = masks_of(self.count)
        self.token = None
        self.state = {}
        self.results = {}

    def bit(self, mask):
        return (self.index // mask) % 2

    def begin(self, name, partial, finish):
        rows, cols = partial.shape
        blocks = partial.reshape(self.count // 2, 2, rows // self.count, cols)
        bit = self.bit(self.masks[0])
        got = swap(pick(blocks, 1 - bit), "dp", self.masks[0])
        self.state[name] = (0, pick(blocks, bit), got, finish)

    def order(self, *arrays):
        if self.token is None:
            self.token = jnp.zeros((8, 128), full)
        *arrays, self.token = lax.optimization_barrier((*arrays, self.token))
        return arrays

    def advance(self, name):
        stage, keep, got, finish = self.state[name]
        steps = len(self.masks)
        keep, got = self.order(keep, got)
        if stage < steps:
            total = keep.astype(full) + got.astype(full)
            if stage < steps - 1:
                total = total.astype(low)
                blocks = total.reshape(total.shape[0] // 2, 2, *total.shape[1:])
                bit = self.bit(self.masks[stage + 1])
                keep, send = self.order(pick(blocks, bit), pick(blocks, 1 - bit))
                got = swap(send, "dp", self.masks[stage + 1])
            else:
                (keep,) = self.order(finish(total[0])[None])
                got = swap(keep, "dp", self.masks[-1])
        else:
            bit = self.bit(self.masks[2 * steps - 1 - stage])
            both = jnp.where(bit == 0, jnp.stack([keep, got], 1), jnp.stack([got, keep], 1))
            keep = both.reshape(-1, *keep.shape[1:])
            (keep,) = self.order(keep)
            if stage == 2 * steps - 1:
                self.results[name] = keep.reshape(-1, keep.shape[-1])
            else:
                got = swap(keep, "dp", self.masks[2 * steps - 2 - stage])
        self.state[name] = (stage + 1, keep, got, finish)


def shards(
    hidden_in, out_grad, seq_counts, segment_ids, proj, proj_master, proj_m, proj_v,
    down, down_master, down_m, down_v, vectors, vec_m, vec_v,
):
    group_count = lax.axis_size("dp")
    section = lax.axis_index("section")
    core, layer = section % 2, section // 2
    width = hidden_in.shape[1]
    seq_len = segment_ids.shape[1]
    slots = segment_ids.shape[0] // 2
    rows = slots * seq_len
    wide = proj.shape[2]
    at_first = layer == 0

    def shape(dims, kind):
        return jax.ShapeDtypeStruct(dims, kind)

    own_w = proj[0]
    other_w = swap(own_w, "section", 1)
    d0 = lax.dynamic_index_in_dim(down, layer, 0, keepdims=False)
    d2 = swap(lax.dynamic_index_in_dim(down, 1 - layer, 0, keepdims=False), "section", 2)
    d1 = swap(d0, "section", 1)
    d3 = swap(d2, "section", 1)
    downs = (d0, d1, d2, d3)
    vec = lax.dynamic_index_in_dim(vectors, layer, 0, keepdims=False)

    own_in = lax.dynamic_slice_in_dim(hidden_in, core * rows, rows, 0)
    own_cot = lax.dynamic_slice_in_dim(out_grad, core * rows, rows, 0)
    docs = lax.dynamic_slice_in_dim(segment_ids, core * slots, slots, 0)
    doc_col = docs.reshape(rows, 1)
    live_count = lax.dynamic_index_in_dim(seq_counts[0], core, 0, keepdims=False)
    scal = jnp.stack([core, section, live_count]).astype(jnp.int32)

    weight_sems = pltpu.SemaphoreType.DMA((2,))
    weight_buf = pltpu.VMEM((width, wide), low)
    flops_one = 2 * rows * width * wide

    def run_first(hidden):
        return call(
            forward_first,
            [
                shape((rows, 3 * width), low), shape((rows, width), low),
                shape((rows, width), full), shape((rows, 1), full), shape((rows, width), low),
                shape((4, rows, width), low), shape((4, rows, width), low),
            ],
            (scal, hidden, docs, doc_col, vec, own_w, other_w),
            [smem, vmem, vmem, vmem, vmem, anywhere, anywhere],
            (weight_buf, weight_buf, weight_sems),
            flops=2 * flops_one, moved=15 << 20,
        )

    def run_second(hidden, act):
        return call(
            functools.partial(forward_second, seq_len=seq_len),
            [shape((rows, width), low), shape((rows, width), full), shape((rows, 1), full)],
            (scal, hidden, act, vec, *downs),
            [smem] + [vmem] * 7,
            flops=flops_one, moved=8 << 20,
        )

    def hop(block, towards):
        route = [(0, 2), (1, 3)] if towards else [(2, 0), (3, 1)]
        return lax.ppermute(block, "section", route)

    first = run_first(own_in)
    h_two = run_second(first[4], first[5])[0]
    layer_in = jnp.where(at_first, own_in, hop(h_two, True))
    qkv, ctx, n_one, r_one, h_one, act, slope = run_first(layer_in)
    h_two, n_two, r_two = run_second(h_one, act)

    def by_core(at_zero, at_one):
        return jnp.where(core == 0, at_zero, at_one)

    kept_left = (by_core(layer_in, h_one), by_core(ctx, h_one), by_core(h_one, h_two))
    sent_left = jnp.stack(
        [by_core(h_one, layer_in), by_core(h_one, ctx), by_core(h_two, h_one)]
    )
    got_left = swap(sent_left, "section", 1)
    act_pairs = act.reshape(2, 2, rows, width)
    act_kept = pick(act_pairs, core)
    act_got = swap(pick(act_pairs, 1 - core), "section", 1)

    def run_back_second(upstream):
        return call(
            functools.partial(backward_second, seq_len=seq_len),
            [
                shape((rows, width), low), shape((4, rows, width), low),
                shape((rows, width), full), shape((8, width), full),
            ],
            (scal, upstream, n_two, r_two, slope, vec, *downs, own_w, other_w),
            [smem] + [vmem] * 9 + [anywhere] * 2,
            (weight_buf, weight_sems),
            flops=2 * flops_one, moved=16 << 20,
        )

    def run_back_first(upstream):
        return call(
            backward_first,
            [shape((4, rows, width), low), shape((rows, width), full), shape((8, width), full)],
            (scal, upstream, n_one, r_one, qkv, docs, doc_col, vec, own_w, other_w),
            [smem] + [vmem] * 7 + [anywhere] * 2,
            (weight_buf, pltpu.VMEM((rows, width), low), weight_sems),
            flops=2 * flops_one, moved=10 << 20,
        )

    def run_down(db):
        return call(
            down_gradient,
            shape((2, width, width), low),
            (act_kept, act_got, db, swap(db, "section", 1)),
            [vmem] * 4,
            flops=2 * flops_one, moved=6 << 20,
        )

    db, dpre, dh_two, sums_two = run_back_second(own_cot)
    dqkvd, dh_one, sums_one = run_back_first(dh_two)
    early_down = run_down(db)
    early = jnp.where(at_first, hop(early_down[0], False), early_down[1])

    upstream = jnp.where(at_first, hop(dh_one.astype(low), False).astype(full), own_cot)
    db, dpre, dh_two, sums_two = run_back_second(upstream)
    late_down = run_down(db)
    late = jnp.where(at_first, late_down[0], hop(late_down[1], True))
    dqkvd, dh_one, sums_one = run_back_first(dh_two)

    kept_right = by_core(dqkvd, dpre)
    got_right = swap(by_core(dpre, dqkvd), "section", 1)
    kept_grad = by_core(dh_one, dh_two)
    got_grad = swap(by_core(dh_two, dh_one), "section", 1)

    moments = {}

    def finish_proj(k):
        cols = slice(k * width, (k + 1) * width)

        def finish(total):
            grad = total / group_count
            new = adam_apply(
                proj_master[0, :, cols], proj_m[0, :, cols], proj_v[0, :, cols], grad, weight_decay
            )
            moments["proj", k] = (grad, *new)
            return new[0].astype(low)

        return finish

    def finish_down(at):
        def finish(total):
            grad = total.T / group_count
            new = adam_apply(down_master[at], down_m[at], down_v[at], grad, weight_decay)
            moments["down", at] = (grad, *new)
            return new[0].astype(low).T

        return finish

    exchange = Exchange()
    stages = 2 * len(exchange.masks)
    exchange.begin("early", early, finish_down(1))
    for _ in range(stages):
        exchange.advance("early")
    names = []
    for k in range(4):
        lhs = 0 if k < 3 else 1
        partial = call(
            weight_gradient,
            shape((width, width), low),
            (kept_left[lhs], got_left[lhs], kept_right[k], got_right[k]),
            [vmem] * 4,
            flops=flops_one // 2, moved=4 << 20,
        )
        exchange.begin(k, partial, finish_proj(k))
        names.append(k)
    exchange.begin("late", late, finish_down(0))
    names.append("late")
    plan = []
    for place, name in enumerate(names):
        at = 13.0 * (place + 1)
        for stage in range(stages - 1):
            plan.append((at, place, name))
            at += 10.5
        plan.append((max(at, 13.0 * (len(names) + place)) + 13.0, place, name))
    for _, _, name in sorted(plan, key=lambda item: item[:2]):
        exchange.advance(name)

    sums = jnp.concatenate([sums_one[:5], sums_two[:7]], 0)
    sums = sums + swap(sums, "section", 1)
    for mask in masks_of(group_count):
        sums = sums + swap(sums, "dp", mask)
    other_sums = swap(sums, "section", 2)
    vec_grad = jnp.where(
        at_first, jnp.stack([sums, other_sums]), jnp.stack([other_sums, sums])
    ) / group_count
    vec_moments = adam_apply(vectors, vec_m, vec_v, vec_grad, 0.0)

    def in_order(kept, got):
        return by_core(jnp.concatenate([kept, got], 0), jnp.concatenate([got, kept], 0))[None]

    proj_parts = [
        jnp.concatenate([moments["proj", k][i] for k in range(4)], 1)[None] for i in range(4)
    ]
    down_parts = [jnp.stack([moments["down", at][i] for at in range(2)]) for i in range(4)]
    proj_copy = jnp.concatenate([exchange.results[k] for k in range(4)], 1)[None]
    down_copy = jnp.stack([exchange.results["late"].T, exchange.results["early"].T])
    return (
        in_order(kept_left[2], got_left[2]),
        in_order(kept_grad, got_grad),
        *proj_parts,
        proj_copy,
        *down_parts,
        down_copy,
        vec_grad,
        vec_moments[1],
        vec_moments[2],
    )


def solution(mesh):
    shared = P("section", "dp", None)
    split = P(None, "section", "dp")
    placed = (
        P("dp", None), P("dp", None), P("dp", None), P("dp", None),
        P("section", None, None), shared, shared, shared,
        P(None, "section", None), split, split, split, P(), P(), P(),
    )
    return jax.shard_map(
        shards,
        mesh=mesh,
        in_specs=placed,
        out_specs=(
            shared, shared, shared, shared, shared, shared,
            P("section", None, None), split, split, split, split,
            P(None, "section", None), P(), P(), P(),
        ),
        check_vma=False,
    )
```

time: 3220 us -> 424 us (0.13); the launches traced: 3180 us -> 418 us
  local copies, waits for them, and re-layouts: 2140 us -> 26.9 us
  waiting for transfers between devices: 776 us -> 192 us
  Pallas kernels: 0 us -> 97.4 us
  matrix products: 69.9 us -> 0 us
  other arithmetic: 97.3 us -> 36.4 us
  loops' own time: 43.9 us -> 0 us
    unnamed x49 -> x75, local copies, waits for them, and re-layouts: 1860 us -> 5.63 us
    psum x2 -> x0, waiting for transfers between devices: 336 us -> none  [the longest x1 230 us: shards(): lax.psum(matrix_local.astype(jnp.bfloat16), 'dp').astype(jnp.float32)]
    all_gather x3 -> x0, waiting for transfers between devices: 197 us -> none  [the longest x1 74 us: shards(): lax.all_gather(proj_new.astype(jnp.bfloat16), 'dp', axis=1, tiled=True)]
    dynamic_update_slice x2 -> x0, local copies, waits for them, and re-layouts: 136 us -> none  [the longest x1 135 us: shards(): lax.dynamic_update_index_in_dim(jnp.zeros(down_whole.shape, jnp.float32),...]
    pallas_call x0 -> x14, Pallas kernels: none -> 97.4 us  [call(): pl.pallas_call(kernel, out_shape=outs, in_specs=specs, out_specs=jax.tree...]
    dot_general x28 -> x0, matrix products: 59.3 us -> none  [the longest x4 13.9 us: attend_forward(): jnp.dot(flat_rows, matrices[:, :3 * model_width], preferred_element_type=...]
    unnamed x7 -> x0, waiting for transfers between devices: 56.7 us -> none
    another operation x36 -> x0, local copies, waits for them, and re-layouts: 47.7 us -> none
  transfers between devices with their start and end apart: 14 -> 55, of which waited for: 14 -> 30; matrix products, arithmetic and copies ran while one was open for 2% -> 14% of each run, Pallas kernels for 0% -> 13%
where the time goes in v1:
time: 424 us; the launch traced here: 418 us
  waiting for transfers between devices  192 us (45%)
  Pallas kernels  97.4 us (23%)
  starting transfers between devices  63.2 us (15%)
  other arithmetic  36.4 us (9%)
  local copies, waits for them, and re-layouts  26.9 us (6%)
    ppermute x51, waiting for transfers between devices, swap(): lax.ppermute(block, axis, [(i, i ^ mask) for i in range(lax.axis_size(axi...  161 us
    pallas_call x14, Pallas kernels, call(): pl.pallas_call(kernel, out_shape=outs, in_specs=specs, out_specs=jax.tree...  97.4 us
    ppermute x51, starting transfers between devices, swap(): lax.ppermute(block, axis, [(i, i ^ mask) for i in range(lax.axis_size(axi...  51.1 us
    ppermute x4, waiting for transfers between devices, hop(): return lax.ppermute(block, 'section', route)  31.1 us
    ppermute x4, starting transfers between devices, hop(): return lax.ppermute(block, 'section', route)  12.1 us
    squeeze x18, local copies, waits for them, and re-layouts, pick(): return lax.dynamic_index_in_dim(block, at, 1, keepdims=False)  9.36 us
  transfers between devices with their start and end apart: 55, of which 30 were waited for; matrix products, arithmetic and copies ran while one was open for 14% of the time, Pallas kernels for 13%

profile of v1, /device:TPU:0, one launch (start us, length us, event | category | flops | bytes accessed | tf_op | source)
XLA Modules:
  0.0 417.9 jit_solution(8777264204697030741)
XLA Ops:
  5.8 26.4 %collective-permute-done.2.d2 = bf16[768,768]{1,0:T(8,128)(2,1)S(1)} collective-permute-done((bf16[768,768]{1,0:T(8,128)(2,1)S(1)}, bf16[768,768]{1,0:T(8,128)(2,1)S(1)}, u32[]{:S(2)}, u32[]{:S(2)}) %collective-permute-start.2) | collective-permute-done | bytes 1179680 | tf_op jit(solution)/shard_map/ppermute | solution.py:285
  36.5 10.7 %shard_map.262 = (bf16[256,2304]{1,0:T(8,128)(2,1)}, bf16[256,768]{1,0:T(8,128)(2,1)}, f32[256,768]{1,0:T(8,128)}, f32[256,1]{1,0:T(8,128)}, bf16[256,768]{1,0:T...) custom-call(s32[3]{0:T(128)} %pad_add_fusion.scal, ...), custom_call_target="tpu_custom_call" | custom-call | flops 2415919104 | bytes 15728640 | tf_op jit(solution)/shard_map/pallas_call | solution.py:67
  47.3 5.7 %shard_map.263 = (bf16[256,768]{1,0:T(8,128)(2,1)}, f32[256,768]{1,0:T(8,128)}, f32[256,1]{1,0:T(8,128)}) custom-call(s32[3]{0:T(128)} %pad_add_fusion.scal, bf16[256,768]{1,0:T(8,128)(2,1)} %get-tuple-element.208.h_ref, bf16[4,256,768]{2,1,0:T(8,128)(2,1)} %get-tuple-element.209.act_ref, f32[12,768]{1,0:T(8,128)} %bitcast.439, bf16[768,768]{1,0:T(8,128)(2,1)} %copy-done.2, ...), custom_call_target="tpu_custom_call" | custom-call | flops 1207959552 | bytes 8388608 | tf_op jit(solution)/shard_map/pallas_call | solution.py:67
  53.1 3.8 collective-permute-start.4
  58.0 7.9 %collective-permute-done.4 = bf16[256,768]{1,0:T(8,128)(2,1)S(1)} collective-permute-done((bf16[256,768]{1,0:T(8,128)(2,1)}, bf16[256,768]{1,0:T(8,128)(2,1)S(1)}, u32[]{:S(2)}, u32[]{:S(2)}) %collective-permute-start.4) | collective-permute-done | bytes 393248 | tf_op jit(solution)/shard_map/ppermute | solution.py:421
  66.7 10.7 %shard_map.264 = (bf16[256,2304]{1,0:T(8,128)(2,1)}, bf16[256,768]{1,0:T(8,128)(2,1)}, f32[256,768]{1,0:T(8,128)}, f32[256,1]{1,0:T(8,128)}, bf16[256,768]{1,0:T...) custom-call(s32[3]{0:T(128)} %pad_add_fusion.scal, ...), custom_call_target="tpu_custom_call" | custom-call | flops 2415919104 | bytes 15728640 | tf_op jit(solution)/shard_map/pallas_call | solution.py:67
  77.5 5.6 %shard_map.265 = (bf16[256,768]{1,0:T(8,128)(2,1)}, f32[256,768]{1,0:T(8,128)}, f32[256,1]{1,0:T(8,128)}) custom-call(s32[3]{0:T(128)} %pad_add_fusion.scal, bf16[256,768]{1,0:T(8,128)(2,1)} %get-tuple-element.211.h_ref, bf16[4,256,768]{2,1,0:T(8,128)(2,1)} %get-tuple-element.212.act_ref, f32[12,768]{1,0:T(8,128)} %bitcast.441, bf16[768,768]{1,0:T(8,128)(2,1)} %copy-done.2, ...), custom_call_target="tpu_custom_call" | custom-call | flops 1207959552 | bytes 8388608 | tf_op jit(solution)/shard_map/pallas_call | solution.py:67
  83.1 8.4 %shard_map.266 = (bf16[256,768]{1,0:T(8,128)(2,1)}, bf16[4,256,768]{2,1,0:T(8,128)(2,1)}, f32[256,768]{1,0:T(8,128)}, f32[8,768]{1,0:T(8,128)}) custom-call(s32[3]{0:T(128)} %pad_add_fusion.scal, f32[256,768]{1,0:T(8,128)} %constant_dynamic-slice_fusion.12.e_ref, f32[256,768]{1,0:T(8,128)} %get-tuple-element.215.n_ref, f32[256,1]{1,0:T(8,128)} %get-tuple-element.216.r_ref, ...), custom_call_target="tpu_custom_call" | custom-call | flops 2415919104 | bytes 16777216 | tf_op jit(solution)/shard_map/pallas_call | solution.py:67
  91.5 13.3 %shard_map.267 = (bf16[4,256,768]{2,1,0:T(8,128)(2,1)}, f32[256,768]{1,0:T(8,128)}, f32[8,768]{1,0:T(8,128)}) custom-call(s32[3]{0:T(128)} %pad_add_fusion.scal, f32[256,768]{1,0:T(8,128)} %get-tuple-element.218.e_ref, f32[256,768]{1,0:T(8,128)} %get-tuple-element.219.n_ref, f32[256,1]{1,0:T(8,128)} %get-tuple-element.220.r_ref, ...), custom_call_target="tpu_custom_call" | custom-call | flops 2415919104 | bytes 10485760 | tf_op jit(solution)/shard_map/pallas_call | solution.py:67
  110.1 8.4 %collective-permute-done.6 = bf16[256,768]{1,0:T(8,128)(2,1)S(1)} collective-permute-done((bf16[256,768]{1,0:T(8,128)(2,1)S(1)}, bf16[256,768]{1,0:T(8,128)(2,1)S(1)}, u32[]{:S(2)}, u32[]{:S(2)}) %collective-permute-start.6) | collective-permute-done | bytes 393248 | tf_op jit(solution)/shard_map/ppermute | solution.py:421
  119.4 8.4 %shard_map.268 = (bf16[256,768]{1,0:T(8,128)(2,1)}, bf16[4,256,768]{2,1,0:T(8,128)(2,1)}, f32[256,768]{1,0:T(8,128)}, f32[8,768]{1,0:T(8,128)}) custom-call(s32[3]{0:T(128)} %pad_add_fusion.scal, f32[256,768]{1,0:T(8,128)} %convert_select_fusion.e_ref, f32[256,768]{1,0:T(8,128)} %get-tuple-element.215.n_ref, f32[256,1]{1,0:T(8,128)} %get-tuple-element.216.r_ref, ...), custom_call_target="tpu_custom_call" | custom-call | flops 2415919104 | bytes 16777216 | tf_op jit(solution)/shard_map/pallas_call | solution.py:67
  127.9 12.7 %shard_map.269 = (bf16[4,256,768]{2,1,0:T(8,128)(2,1)}, f32[256,768]{1,0:T(8,128)}, f32[8,768]{1,0:T(8,128)}) custom-call(s32[3]{0:T(128)} %pad_add_fusion.scal, f32[256,768]{1,0:T(8,128)} %get-tuple-element.223.e_ref, f32[256,768]{1,0:T(8,128)} %get-tuple-element.219.n_ref, f32[256,1]{1,0:T(8,128)} %get-tuple-element.220.r_ref, ...), custom_call_target="tpu_custom_call" | custom-call | flops 2415919104 | bytes 10485760 | tf_op jit(solution)/shard_map/pallas_call | solution.py:67
  156.7 4.6 %shard_map.271 = bf16[2,768,768]{2,1,0:T(8,128)(2,1)} custom-call(bf16[2,256,768]{2,1,0:T(8,128)(2,1)} %get-tuple-element.475.act_own, bf16[2,256,768]{2,1,0:T(8,128)(2,1)} %collective-permute-done.10.act_other, bf16[256,768]{1,0:T(8,128)(2,1)} %get-tuple-element.227.db_own, bf16[256,768]{1,0:T(8,128)(2,1)} %collective-permute-done.11.db_other), custom_call_target="tpu_custom_call" | custom-call | flops 2415919104 | bytes 6291456 | tf_op jit(solution)/shard_map/pallas_call | solution.py:67
  164.0 4.4 %shard_map.275 = bf16[2,768,768]{2,1,0:T(8,128)(2,1)} custom-call(bf16[2,256,768]{2,1,0:T(8,128)(2,1)} %get-tuple-element.475.act_own, bf16[2,256,768]{2,1,0:T(8,128)(2,1)} %collective-permute-done.10.act_other, bf16[256,768]{1,0:T(8,128)(2,1)} %get-tuple-element.335.db_own, bf16[256,768]{1,0:T(8,128)(2,1)} %collective-permute-done.35.db_other), custom_call_target="tpu_custom_call" | custom-call | flops 2415919104 | bytes 6291456 | tf_op jit(solution)/shard_map/pallas_call | solution.py:67
  169.8 5.7 %collective-permute-start.36 = (bf16[768,768]{1,0:T(8,128)(2,1)S(1)}, bf16[768,768]{1,0:T(8,128)(2,1)S(1)}, u32[]{:S(2)}, u32[]{:S(2)}) collective-permute-start(bf16[768,768]{1,0:T(8,128)(2,1)S(1)} %slice_bitcast_fusion.2), channel_id=1, source_target_pairs={{0,2},{1,3},{4,6},{5,7},{8,10},{9,11},{12,14},{13,15},{16,18},{17,... | collective-permute-start | bytes 3538952 | tf_op jit(solution)/shard_map/ppermute | solution.py:421
  182.5 10.1 %collective-permute-done.12 = bf16[768,768]{1,0:T(8,128)(2,1)} collective-permute-done((bf16[768,768]{1,0:T(8,128)(2,1)S(1)}, bf16[768,768]{1,0:T(8,128)(2,1)}, u32[]{:S(2)}, u32[]{:S(2)}) %collective-permute-start.12) | collective-permute-done | bytes 1179680 | tf_op jit(solution)/shard_map/ppermute | solution.py:421
  195.8 4.8 %collective-permute-done.36 = bf16[768,768]{1,0:T(8,128)(2,1)S(1)} collective-permute-done((bf16[768,768]{1,0:T(8,128)(2,1)S(1)}, bf16[768,768]{1,0:T(8,128)(2,1)S(1)}, u32[]{:S(2)}, u32[]{:S(2)}) %collective-permute-start.36) | collective-permute-done | bytes 1179680 | tf_op jit(solution)/shard_map/ppermute | solution.py:421
  206.7 3.8 collective-permute-done.13
  210.6 10.7 %collective-permute-done.37 = bf16[4,96,768]{2,1,0:T(8,128)(2,1)S(1)} collective-permute-done((bf16[4,96,768]{2,1,0:T(8,128)(2,1)S(1)}, bf16[4,96,768]{2,1,0:T(8,128)(2,1)S(1)}, u32[]{:S(2)}, u32[]{:S(2)}) %collective-permute-start.37) | collective-permute-done | bytes 589856 | tf_op jit(solution)/shard_map/ppermute | solution.py:285
  234.3 5.3 %collective-permute-done.39 = bf16[2,96,768]{2,1,0:T(8,128)(2,1)S(1)} collective-permute-done((bf16[2,96,768]{2,1,0:T(8,128)(2,1)S(1)}, bf16[2,96,768]{2,1,0:T(8,128)(2,1)S(1)}, u32[]{:S(2)}, u32[]{:S(2)}) %collective-permute-start.39) | collective-permute-done | bytes 294944 | tf_op jit(solution)/shard_map/ppermute | solution.py:285
  264.4 3.6 collective-permute-done.17
  271.5 7.3 %collective-permute-done.48 = bf16[2,96,768]{2,1,0:T(8,128)(2,1)S(1)} collective-permute-done((bf16[2,96,768]{2,1,0:T(8,128)(2,1)S(1)}, bf16[2,96,768]{2,1,0:T(8,128)(2,1)S(1)}, u32[]{:S(2)}, u32[]{:S(2)}) %collective-permute-start.48) | collective-permute-done | bytes 294944 | tf_op jit(solution)/shard_map/ppermute | solution.py:285
  279.3 5.4 %collective-permute-done.18 = bf16[4,96,768]{2,1,0:T(8,128)(2,1)S(1)} collective-permute-done((bf16[4,96,768]{2,1,0:T(8,128)(2,1)S(1)}, bf16[4,96,768]{2,1,0:T(8,128)(2,1)S(1)}, u32[]{:S(2)}, u32[]{:S(2)}) %collective-permute-start.18) | collective-permute-done | bytes 589856 | tf_op jit(solution)/shard_map/ppermute | solution.py:285
  289.0 19.8 %collective-permute-done.49 = bf16[4,96,768]{2,1,0:T(8,128)(2,1)S(1)} collective-permute-done((bf16[4,96,768]{2,1,0:T(8,128)(2,1)S(1)}, bf16[4,96,768]{2,1,0:T(8,128)(2,1)S(1)}, u32[]{:S(2)}, u32[]{:S(2)}) %collective-permute-start.49) | collective-permute-done | bytes 589856 | tf_op jit(solution)/shard_map/ppermute | solution.py:285
  327.1 5.2 %collective-permute-done.24 = bf16[1,96,768]{2,1,0:T(8,128)(2,1)S(1)} collective-permute-done((bf16[1,96,768]{2,1,0:T(8,128)(2,1)S(1)}, bf16[1,96,768]{2,1,0:T(8,128)(2,1)S(1)}, u32[]{:S(2)}, u32[]{:S(2)}) %collective-permute-start.24) | collective-permute-done | bytes 147488 | tf_op jit(solution)/shard_map/ppermute | solution.py:285
  334.8 10.6 %collective-permute-done.26 = bf16[2,96,768]{2,1,0:T(8,128)(2,1)S(1)} collective-permute-done((bf16[2,96,768]{2,1,0:T(8,128)(2,1)S(1)}, bf16[2,96,768]{2,1,0:T(8,128)(2,1)S(1)}, u32[]{:S(2)}, u32[]{:S(2)}) %collective-permute-start.26) | collective-permute-done | bytes 294944 | tf_op jit(solution)/shard_map/ppermute | solution.py:285
  352.9 4.0 collective-permute-done.27
  358.0 11.7 %collective-permute-done.31 = bf16[2,96,768]{2,1,0:T(8,128)(2,1)S(1)} collective-permute-done((bf16[2,96,768]{2,1,0:T(8,128)(2,1)S(1)}, bf16[2,96,768]{2,1,0:T(8,128)(2,1)S(1)}, u32[]{:S(2)}, u32[]{:S(2)}) %collective-permute-start.31) | collective-permute-done | bytes 294944 | tf_op jit(solution)/shard_map/ppermute | solution.py:285
  381.4 4.7 %collective-permute-done.43 = bf16[1,96,768]{2,1,0:T(8,128)(2,1)S(1)} collective-permute-done((bf16[1,96,768]{2,1,0:T(8,128)(2,1)S(1)}, bf16[1,96,768]{2,1,0:T(8,128)(2,1)S(1)}, u32[]{:S(2)}, u32[]{:S(2)}) %collective-permute-start.43) | collective-permute-done | bytes 147488 | tf_op jit(solution)/shard_map/ppermute | solution.py:285
  389.5 3.9 collective-permute-done.44
  398.2 5.6 %collective-permute-done.42 = bf16[4,96,768]{2,1,0:T(8,128)(2,1)S(1)} collective-permute-done((bf16[4,96,768]{2,1,0:T(8,128)(2,1)S(1)}, bf16[4,96,768]{2,1,0:T(8,128)(2,1)S(1)}, u32[]{:S(2)}, u32[]{:S(2)}) %collective-permute-start.42) | collective-permute-done | bytes 589856 | tf_op jit(solution)/shard_map/ppermute | solution.py:285
  404.1 10.8 %collective-permute-done.45 = bf16[4,96,768]{2,1,0:T(8,128)(2,1)S(1)} collective-permute-done((bf16[4,96,768]{2,1,0:T(8,128)(2,1)S(1)}, bf16[4,96,768]{2,1,0:T(8,128)(2,1)S(1)}, u32[]{:S(2)}, u32[]{:S(2)}) %collective-permute-start.45) | collective-permute-done | bytes 589856 | tf_op jit(solution)/shard_map/ppermute | solution.py:285
  (275 shorter events, 151.7 us)
Async XLA Ops:
  0.7 35.9 %collective-permute-start = (bf16[768,3072]{1,0:T(8,128)(2,1)}, bf16[768,3072]{1,0:T(8,128)(2,1)}, u32[]{:S(2)}, u32[]{:S(2)}) collective-permute-start(bf16[768,3072]{1,0:T(8,128)(2,1)} %bitcast.418), channel_id=1, source_target_pairs={{0,1},{1,0},{2,3},{3,2},{4,5},{5,4},{6,7},{7,6},{8,9},{9,8},{10,11... | collective-permute-start | bytes 14155784 | tf_op jit(solution)/shard_map/ppermute | solution.py:285
  3.1 29.2 %collective-permute-start.2 = (bf16[768,768]{1,0:T(8,128)(2,1)S(1)}, bf16[768,768]{1,0:T(8,128)(2,1)S(1)}, u32[]{:S(2)}, u32[]{:S(2)}) collective-permute-start(bf16[768,768]{1,0:T(8,128)(2,1)S(1)} %get-tuple-element.470), channel_id=1, source_target_pairs={{0,2},{1,3},{2,0},{3,1},{4,6},{5,7},{6,4},{7,5},{8,10},{9,11},{10,... | collective-permute-start | bytes 3538952 | tf_op jit(solution)/shard_map/ppermute | solution.py:285
  5.7 41.6 %collective-permute-start.1 = (bf16[768,768]{1,0:T(8,128)(2,1)S(1)}, bf16[768,768]{1,0:T(8,128)(2,1)}, u32[]{:S(2)}, u32[]{:S(2)}) collective-permute-start(bf16[768,768]{1,0:T(8,128)(2,1)S(1)} %get-tuple-element.471.d0), channel_id=1, source_target_pairs={{0,1},{1,0},{2,3},{3,2},{4,5},{5,4},{6,7},{7,6},{8,9},{9,8},{10,11... | collective-permute-start | bytes 3538952 | tf_op jit(solution)/shard_map/ppermute | solution.py:285
  32.3 15.1 %collective-permute-start.3 = (bf16[768,768]{1,0:T(8,128)(2,1)S(1)}, bf16[768,768]{1,0:T(8,128)(2,1)}, u32[]{:S(2)}, u32[]{:S(2)}) collective-permute-start(bf16[768,768]{1,0:T(8,128)(2,1)S(1)} %collective-permute-done.2.d2), channel_id=1, source_target_pairs={{0,1},{1,0},{2,3},{3,2},{4,5},{5,4},{6,7},{7,6},{8,9},{9,8},{10,11... | collective-permute-start | bytes 3538952 | tf_op jit(solution)/shard_map/ppermute | solution.py:285
  107.4 48.7 %collective-permute-start.11 = (bf16[256,768]{1,0:T(8,128)(2,1)S(1)}, bf16[256,768]{1,0:T(8,128)(2,1)}, u32[]{:S(2)}, u32[]{:S(2)}) collective-permute-start(bf16[256,768]{1,0:T(8,128)(2,1)S(1)} %copy-done.33), channel_id=1, source_target_pairs={{0,1},{1,0},{2,3},{3,2},{4,5},{5,4},{6,7},{7,6},{8,9},{9,8},{10,11... | collective-permute-start | bytes 1179656 | tf_op jit(solution)/shard_map/ppermute | solution.py:285
  108.5 48.2 %collective-permute-start.10 = (bf16[2,256,768]{2,1,0:T(8,128)(2,1)S(1)}, bf16[2,256,768]{2,1,0:T(8,128)(2,1)}, u32[]{:S(2)}, u32[]{:S(2)}) collective-permute-start(bf16[2,256,768]{2,1,0:T(8,128)(2,1)S(1)} %get-tuple-element.474), channel_id=1, source_target_pairs={{0,1},{1,0},{2,3},{3,2},{4,5},{5,4},{6,7},{7,6},{8,9},{9,8},{10,11... | collective-permute-start | bytes 2359304 | tf_op jit(solution)/shard_map/ppermute | solution.py:285
  141.6 35.9 %collective-permute-start.5 = (bf16[3,256,768]{2,1,0:T(8,128)(2,1)S(1)}, bf16[3,256,768]{2,1,0:T(8,128)(2,1)S(1)}, u32[]{:S(2)}, u32[]{:S(2)}) collective-permute-start(bf16[3,256,768]{2,1,0:T(8,128)(2,1)S(1)} %pad_maximum_fusion.1), channel_id=1, source_target_pairs={{0,1},{1,0},{2,3},{3,2},{4,5},{5,4},{6,7},{7,6},{8,9},{9,8},{10,11... | collective-permute-start | bytes 3538952 | tf_op jit(solution)/shard_map/ppermute | solution.py:285
  142.2 20.5 %collective-permute-start.35 = (bf16[256,768]{1,0:T(8,128)(2,1)}, bf16[256,768]{1,0:T(8,128)(2,1)}, u32[]{:S(2)}, u32[]{:S(2)}) collective-permute-start(bf16[256,768]{1,0:T(8,128)(2,1)} %get-tuple-element.335.db_own), channel_id=1, source_target_pairs={{0,1},{1,0},{2,3},{3,2},{4,5},{5,4},{6,7},{7,6},{8,9},{9,8},{10,11... | collective-permute-start | bytes 1179656 | tf_op jit(solution)/shard_map/ppermute | solution.py:285
  156.1 46.3 %collective-permute-start.8 = (bf16[4,256,768]{2,1,0:T(8,128)(2,1)S(1)}, bf16[4,256,768]{2,1,0:T(8,128)(2,1)S(1)}, u32[]{:S(2)}, u32[]{:S(2)}) collective-permute-start(bf16[4,256,768]{2,1,0:T(8,128)(2,1)S(1)} %get-tuple-element.468), channel_id=1, source_target_pairs={{0,1},{1,0},{2,3},{3,2},{4,5},{5,4},{6,7},{7,6},{8,9},{9,8},{10,11... | collective-permute-start | bytes 4718600 | tf_op jit(solution)/shard_map/ppermute | solution.py:285
  156.1 23.6 %collective-permute-start.7 = (f32[256,768]{1,0:T(8,128)}, f32[256,768]{1,0:T(8,128)}, u32[]{:S(2)}, u32[]{:S(2)}) collective-permute-start(f32[256,768]{1,0:T(8,128)} %get-tuple-element.485), channel_id=1, source_target_pairs={{0,1},{1,0},{2,3},{3,2},{4,5},{5,4},{6,7},{7,6},{8,9},{9,8},{10,11... | collective-permute-start | bytes 2359304 | tf_op jit(solution)/shard_map/ppermute | solution.py:285
  162.7 30.0 %collective-permute-start.12 = (bf16[768,768]{1,0:T(8,128)(2,1)S(1)}, bf16[768,768]{1,0:T(8,128)(2,1)}, u32[]{:S(2)}, u32[]{:S(2)}) collective-permute-start(bf16[768,768]{1,0:T(8,128)(2,1)S(1)} %slice_bitcast_fusion.1), channel_id=1, source_target_pairs={{2,0},{3,1},{6,4},{7,5},{10,8},{11,9},{14,12},{15,13},{18,16},{19,... | collective-permute-start | bytes 3538952 | tf_op jit(solution)/shard_map/ppermute | solution.py:421
  169.8 30.8 %collective-permute-start.36 = (bf16[768,768]{1,0:T(8,128)(2,1)S(1)}, bf16[768,768]{1,0:T(8,128)(2,1)S(1)}, u32[]{:S(2)}, u32[]{:S(2)}) collective-permute-start(bf16[768,768]{1,0:T(8,128)(2,1)S(1)} %slice_bitcast_fusion.2), channel_id=1, source_target_pairs={{0,2},{1,3},{4,6},{5,7},{8,10},{9,11},{12,14},{13,15},{16,18},{17,... | collective-permute-start | bytes 3538952 | tf_op jit(solution)/shard_map/ppermute | solution.py:421
  194.2 16.3 %collective-permute-start.13 = (bf16[4,96,768]{2,1,0:T(8,128)(2,1)S(1)}, bf16[4,96,768]{2,1,0:T(8,128)(2,1)S(1)}, u32[]{:S(2)}, u32[]{:S(2)}) collective-permute-start(bf16[4,96,768]{2,1,0:T(8,128)(2,1)S(1)} %get-tuple-element.488), channel_id=1, source_target_pairs={{0,4},{4,0},{8,12},{12,8},{16,20},{20,16},{24,28},{28,24},{1,5},{5... | collective-permute-start | bytes 1769480 | tf_op jit(solution)/shard_map/ppermute | solution.py:285
  200.8 20.6 %collective-permute-start.37 = (bf16[4,96,768]{2,1,0:T(8,128)(2,1)S(1)}, bf16[4,96,768]{2,1,0:T(8,128)(2,1)S(1)}, u32[]{:S(2)}, u32[]{:S(2)}) collective-permute-start(bf16[4,96,768]{2,1,0:T(8,128)(2,1)S(1)} %get-tuple-element.486), channel_id=1, source_target_pairs={{0,4},{4,0},{8,12},{12,8},{16,20},{20,16},{24,28},{28,24},{1,5},{5... | collective-permute-start | bytes 1769480 | tf_op jit(solution)/shard_map/ppermute | solution.py:285
  223.4 63.7 %collective-permute-start.9 = (bf16[4,96,768]{2,1,0:T(8,128)(2,1)S(1)}, bf16[4,96,768]{2,1,0:T(8,128)(2,1)S(1)}, u32[]{:S(2)}, u32[]{:S(2)}) collective-permute-start(bf16[4,96,768]{2,1,0:T(8,128)(2,1)S(1)} %get-tuple-element.490), channel_id=1, source_target_pairs={{0,4},{4,0},{8,12},{12,8},{16,20},{20,16},{24,28},{28,24},{1,5},{5... | collective-permute-start | bytes 1769480 | tf_op jit(solution)/shard_map/ppermute | solution.py:285
  229.4 80.6 %collective-permute-start.21 = (bf16[4,96,768]{2,1,0:T(8,128)(2,1)S(1)}, bf16[4,96,768]{2,1,0:T(8,128)(2,1)S(1)}, u32[]{:S(2)}, u32[]{:S(2)}) collective-permute-start(bf16[4,96,768]{2,1,0:T(8,128)(2,1)S(1)} %get-tuple-element.492), channel_id=1, source_target_pairs={{0,4},{4,0},{8,12},{12,8},{16,20},{20,16},{24,28},{28,24},{1,5},{5... | collective-permute-start | bytes 1769480 | tf_op jit(solution)/shard_map/ppermute | solution.py:285
  231.2 17.6 %collective-permute-start.15 = (bf16[1,96,768]{2,1,0:T(8,128)(2,1)S(1)}, bf16[1,96,768]{2,1,0:T(8,128)(2,1)S(1)}, u32[]{:S(2)}, u32[]{:S(2)}) collective-permute-start(bf16[1,96,768]{2,1,0:T(8,128)(2,1)S(1)} %get-tuple-element.238), channel_id=1, source_target_pairs={{0,16},{4,20},{8,24},{12,28},{16,0},{20,4},{24,8},{28,12},{1,17},{... | collective-permute-start | bytes 442376 | tf_op jit(solution)/shard_map/ppermute | solution.py:285
  247.3 76.7 %collective-permute-start.25 = (bf16[4,96,768]{2,1,0:T(8,128)(2,1)}, bf16[4,96,768]{2,1,0:T(8,128)(2,1)}, u32[]{:S(2)}, u32[]{:S(2)}) collective-permute-start(bf16[4,96,768]{2,1,0:T(8,128)(2,1)} %get-tuple-element.494), channel_id=1, source_target_pairs={{0,4},{4,0},{8,12},{12,8},{16,20},{20,16},{24,28},{28,24},{1,5},{5... | collective-permute-start | bytes 1769480 | tf_op jit(solution)/shard_map/ppermute | solution.py:285
  268.1 16.6 %collective-permute-start.18 = (bf16[4,96,768]{2,1,0:T(8,128)(2,1)S(1)}, bf16[4,96,768]{2,1,0:T(8,128)(2,1)S(1)}, u32[]{:S(2)}, u32[]{:S(2)}) collective-permute-start(bf16[4,96,768]{2,1,0:T(8,128)(2,1)S(1)} %bitcast.456), channel_id=1, source_target_pairs={{0,4},{4,0},{8,12},{12,8},{16,20},{20,16},{24,28},{28,24},{1,5},{5... | collective-permute-start | bytes 1769480 | tf_op jit(solution)/shard_map/ppermute | solution.py:285
  278.8 66.7 %collective-permute-start.30 = (bf16[4,96,768]{2,1,0:T(8,128)(2,1)}, bf16[4,96,768]{2,1,0:T(8,128)(2,1)}, u32[]{:S(2)}, u32[]{:S(2)}) collective-permute-start(bf16[4,96,768]{2,1,0:T(8,128)(2,1)} %get-tuple-element.499), channel_id=1, source_target_pairs={{0,4},{4,0},{8,12},{12,8},{16,20},{20,16},{24,28},{28,24},{1,5},{5... | collective-permute-start | bytes 1769480 | tf_op jit(solution)/shard_map/ppermute | solution.py:285
  284.7 24.2 %collective-permute-start.49 = (bf16[4,96,768]{2,1,0:T(8,128)(2,1)S(1)}, bf16[4,96,768]{2,1,0:T(8,128)(2,1)S(1)}, u32[]{:S(2)}, u32[]{:S(2)}) collective-permute-start(bf16[4,96,768]{2,1,0:T(8,128)(2,1)S(1)} %bitcast.454), channel_id=1, source_target_pairs={{0,4},{4,0},{8,12},{12,8},{16,20},{20,16},{24,28},{28,24},{1,5},{5... | collective-permute-start | bytes 1769480 | tf_op jit(solution)/shard_map/ppermute | solution.py:285
  287.2 21.9 %collective-permute-start.19 = (bf16[2,96,768]{2,1,0:T(8,128)(2,1)S(1)}, bf16[2,96,768]{2,1,0:T(8,128)(2,1)S(1)}, u32[]{:S(2)}, u32[]{:S(2)}) collective-permute-start(bf16[2,96,768]{2,1,0:T(8,128)(2,1)S(1)} %get-tuple-element.263), channel_id=1, source_target_pairs={{0,8},{4,12},{8,0},{12,4},{16,24},{20,28},{24,16},{28,20},{1,9},{5... | collective-permute-start | bytes 884744 | tf_op jit(solution)/shard_map/ppermute | solution.py:285
  332.3 17.4 %collective-permute-start.29 = (bf16[2,96,768]{2,1,0:T(8,128)(2,1)S(1)}, bf16[2,96,768]{2,1,0:T(8,128)(2,1)S(1)}, u32[]{:S(2)}, u32[]{:S(2)}) collective-permute-start(bf16[2,96,768]{2,1,0:T(8,128)(2,1)S(1)} %maximum_select_fusion.15), channel_id=1, source_target_pairs={{0,8},{4,12},{8,0},{12,4},{16,24},{20,28},{24,16},{28,20},{1,9},{5... | collective-permute-start | bytes 884744 | tf_op jit(solution)/shard_map/ppermute | solution.py:285
  334.7 16.0 %collective-permute-start.28 = (bf16[1,96,768]{2,1,0:T(8,128)(2,1)S(1)}, bf16[1,96,768]{2,1,0:T(8,128)(2,1)S(1)}, u32[]{:S(2)}, u32[]{:S(2)}) collective-permute-start(bf16[1,96,768]{2,1,0:T(8,128)(2,1)S(1)} %get-tuple-element.318), channel_id=1, source_target_pairs={{0,16},{4,20},{8,24},{12,28},{16,0},{20,4},{24,8},{28,12},{1,17},{... | collective-permute-start | bytes 442376 | tf_op jit(solution)/shard_map/ppermute | solution.py:285
  349.9 47.8 %collective-permute-start.38 = (bf16[4,96,768]{2,1,0:T(8,128)(2,1)S(1)}, bf16[4,96,768]{2,1,0:T(8,128)(2,1)S(1)}, u32[]{:S(2)}, u32[]{:S(2)}) collective-permute-start(bf16[4,96,768]{2,1,0:T(8,128)(2,1)S(1)} %bitcast.446), channel_id=1, source_target_pairs={{0,4},{4,0},{8,12},{12,8},{16,20},{20,16},{24,28},{28,24},{1,5},{5... | collective-permute-start | bytes 1769480 | tf_op jit(solution)/shard_map/ppermute | solution.py:285
  350.8 19.0 %collective-permute-start.34 = (bf16[2,96,768]{2,1,0:T(8,128)(2,1)S(1)}, bf16[2,96,768]{2,1,0:T(8,128)(2,1)S(1)}, u32[]{:S(2)}, u32[]{:S(2)}) collective-permute-start(bf16[2,96,768]{2,1,0:T(8,128)(2,1)S(1)} %maximum_select_fusion.16), channel_id=1, source_target_pairs={{0,8},{4,12},{8,0},{12,4},{16,24},{20,28},{24,16},{28,20},{1,9},{5... | collective-permute-start | bytes 884744 | tf_op jit(solution)/shard_map/ppermute | solution.py:285
  351.2 18.5 %collective-permute-start.31 = (bf16[2,96,768]{2,1,0:T(8,128)(2,1)S(1)}, bf16[2,96,768]{2,1,0:T(8,128)(2,1)S(1)}, u32[]{:S(2)}, u32[]{:S(2)}) collective-permute-start(bf16[2,96,768]{2,1,0:T(8,128)(2,1)S(1)} %get-tuple-element.325), channel_id=1, source_target_pairs={{0,8},{4,12},{8,0},{12,4},{16,24},{20,28},{24,16},{28,20},{1,9},{5... | collective-permute-start | bytes 884744 | tf_op jit(solution)/shard_map/ppermute | solution.py:285
  357.2 14.1 %collective-permute-start.33 = (bf16[1,96,768]{2,1,0:T(8,128)(2,1)S(1)}, bf16[1,96,768]{2,1,0:T(8,128)(2,1)S(1)}, u32[]{:S(2)}, u32[]{:S(2)}) collective-permute-start(bf16[1,96,768]{2,1,0:T(8,128)(2,1)S(1)} %get-tuple-element.345), channel_id=1, source_target_pairs={{0,16},{4,20},{8,24},{12,28},{16,0},{20,4},{24,8},{28,12},{1,17},{... | collective-permute-start | bytes 442376 | tf_op jit(solution)/shard_map/ppermute | solution.py:285
  370.1 27.9 %collective-permute-start.40 = (bf16[4,96,768]{2,1,0:T(8,128)(2,1)S(1)}, bf16[4,96,768]{2,1,0:T(8,128)(2,1)S(1)}, u32[]{:S(2)}, u32[]{:S(2)}) collective-permute-start(bf16[4,96,768]{2,1,0:T(8,128)(2,1)S(1)} %bitcast.448), channel_id=1, source_target_pairs={{0,4},{4,0},{8,12},{12,8},{16,20},{20,16},{24,28},{28,24},{1,5},{5... | collective-permute-start | bytes 1769480 | tf_op jit(solution)/shard_map/ppermute | solution.py:285
  371.3 16.0 %collective-permute-start.41 = (bf16[2,96,768]{2,1,0:T(8,128)(2,1)S(1)}, bf16[2,96,768]{2,1,0:T(8,128)(2,1)S(1)}, u32[]{:S(2)}, u32[]{:S(2)}) collective-permute-start(bf16[2,96,768]{2,1,0:T(8,128)(2,1)S(1)} %maximum_select_fusion.17), channel_id=1, source_target_pairs={{0,8},{4,12},{8,0},{12,4},{16,24},{20,28},{24,16},{28,20},{1,9},{5... | collective-permute-start | bytes 884744 | tf_op jit(solution)/shard_map/ppermute | solution.py:285
  387.5 16.3 %collective-permute-start.42 = (bf16[4,96,768]{2,1,0:T(8,128)(2,1)S(1)}, bf16[4,96,768]{2,1,0:T(8,128)(2,1)S(1)}, u32[]{:S(2)}, u32[]{:S(2)}) collective-permute-start(bf16[4,96,768]{2,1,0:T(8,128)(2,1)S(1)} %bitcast.450), channel_id=1, source_target_pairs={{0,4},{4,0},{8,12},{12,8},{16,20},{20,16},{24,28},{28,24},{1,5},{5... | collective-permute-start | bytes 1769480 | tf_op jit(solution)/shard_map/ppermute | solution.py:285
  393.5 21.4 %collective-permute-start.45 = (bf16[4,96,768]{2,1,0:T(8,128)(2,1)S(1)}, bf16[4,96,768]{2,1,0:T(8,128)(2,1)S(1)}, u32[]{:S(2)}, u32[]{:S(2)}) collective-permute-start(bf16[4,96,768]{2,1,0:T(8,128)(2,1)S(1)} %bitcast.452), channel_id=1, source_target_pairs={{0,4},{4,0},{8,12},{12,8},{16,20},{20,16},{24,28},{28,24},{1,5},{5... | collective-permute-start | bytes 1769480 | tf_op jit(solution)/shard_map/ppermute | solution.py:285
  (58 other events, 565.7 us)
